TPU v7x, 32 devices: a whole 2x2x4 slice. The times are simulated.
32 devices in a mesh: out: 16 (over z, x, core), in: 2 (over y).
Axes of the slice: x: 2, y: 2, z: 4, core: 2. Of those that a mesh axis runs over, the one named last changes fastest.
Arguments:
- slopes: bfloat16 [128, 163840], P('out', 'in'), may hold values from -6 to 6
- cols_first: int32 [128, 16], P(None, 'in'), may hold values from 0 to 319
- count_first: int32 [128, 2], P('out', 'in'), may hold values from 1 to 8
- weight_first: bfloat16 [128, 16, 256, 256], P('out', 'in'), may hold values from -0.125 to 0.125
- bias_first: float32 [32768], P(('out', 'in')), may hold values from -3 to 3
- cols_second: int32 [128, 8], P('out', 'in'), may hold values from 0 to 63
- count_second: int32 [128, 2], P('out', 'in'), may hold values from 1 to 4
- weight_second: bfloat16 [128, 8, 256, 256], P('out', 'in'), may hold values from -0.1875 to 0.1875
- bias_second: float32 [32768], P(('out', 'in')), may hold values from -3 to 3
- cotangent: bfloat16 [128, 32768], P(None, ('out', 'in')), may hold values from -6 to 6
Outputs:
- estimate: bfloat16 [128, 32768], P(None, ('out', 'in'))
- grad_first: bfloat16 [128, 16, 256, 256], P('out', 'in')
- grad_second: bfloat16 [128, 8, 256, 256], P('out', 'in')
Inputs may be any that keep to these rules, and one draw needn't show every extreme that they name: `cols_first`: A local block index within the range of slopes of the slot's in index. `count_first`: slots of a block row at or after this count, within one in range, are not used. `cols_second`: A local block index within the range of reordered hidden units of the slot's in index. `count_second`: slots of a block row at or after this count, within one in range, are not used.
All inputs are finite; a program needn't handle non-finite values.
Results may differ from a plain program's by a relative error of at most 0.025.
Values may be sent and summed in bfloat16 or wider, within the bound.
A program may use at most 128 MiB of HBM per device.

v0:
```python
import jax
import jax.numpy as jnp
from jax import lax
from jax.sharding import PartitionSpec as P

BLK = 256
KD1 = 8
KD2 = 4


def shards(
    slopes,
    cols_first,
    count_first,
    weight_first,
    bias_first,
    cols_second,
    count_second,
    weight_second,
    bias_second,
    cotangent,
):
    rows = weight_first.shape[0]
    live_first = jnp.arange(KD1, dtype=jnp.int32)[None, :] < count_first
    live_second = jnp.arange(KD2, dtype=jnp.int32)[None, :] < count_second
    masked_first = weight_first * live_first.astype(jnp.bfloat16)[:, :, None, None]
    masked_second = weight_second * live_second.astype(jnp.bfloat16)[:, :, None, None]
    gathered = lax.all_gather(slopes, "out", axis=0, tiled=True)
    frames = gathered.shape[0]
    slope_blocks = gathered.reshape(frames, -1, BLK)
    own_cols = lax.dynamic_slice_in_dim(cols_first, lax.axis_index("out") * rows, rows, 0)
    panels_first = jnp.take(slope_blocks, own_cols.reshape(-1), axis=1).reshape(
        frames, rows, KD1, BLK
    )
    partial_first = jnp.einsum(
        "frkb,rkbo->fro", panels_first, masked_first, preferred_element_type=jnp.float32
    ).reshape(frames, rows * BLK)
    summed_first = lax.psum_scatter(partial_first, "in", scatter_dimension=1, tiled=True)
    hidden_first = jnp.tanh(summed_first + bias_first[None, :]).astype(jnp.bfloat16)
    second_input = lax.all_gather(hidden_first, "out", axis=1, tiled=True)
    hidden_blocks = second_input.reshape(frames, -1, BLK)
    panels_second = jnp.take(hidden_blocks, cols_second.reshape(-1), axis=1).reshape(
        frames, rows, KD2, BLK
    )
    partial_second = jnp.einsum(
        "frkb,rkbo->fro", panels_second, masked_second, preferred_element_type=jnp.float32
    ).reshape(frames, rows * BLK)
    summed_second = lax.psum_scatter(partial_second, "in", scatter_dimension=1, tiled=True)
    estimate = jnp.tanh(summed_second + bias_second[None, :]).astype(jnp.bfloat16)
    est32 = estimate.astype(jnp.float32)
    delta_second = (cotangent.astype(jnp.float32) * (1.0 - est32 * est32)).astype(jnp.bfloat16)
    rows_second = lax.all_gather(delta_second, "in", axis=1, tiled=True).reshape(frames, rows, BLK)
    grad_second = jnp.einsum(
        "frkb,fro->rkbo", panels_second, rows_second, preferred_element_type=jnp.float32
    )
    grad_second = (grad_second * live_second.astype(jnp.float32)[:, :, None, None]).astype(
        jnp.bfloat16
    )
    adjoint = jnp.einsum(
        "fro,rkbo->frkb", rows_second, masked_second, preferred_element_type=jnp.float32
    ).reshape(frames, rows * KD2, BLK)
    selector = (
        cols_second.reshape(-1)[:, None]
        == jnp.arange(hidden_blocks.shape[1], dtype=jnp.int32)[None, :]
    ).astype(jnp.float32)
    spread = jnp.einsum("fjb,jc->fcb", adjoint, selector, precision=lax.Precision.HIGHEST).reshape(
        frames, -1
    )
    back_first = lax.psum_scatter(
        spread.astype(jnp.bfloat16), "out", scatter_dimension=1, tiled=True
    ).astype(jnp.float32)
    hid32 = hidden_first.astype(jnp.float32)
    delta_first = (back_first * (1.0 - hid32 * hid32)).astype(jnp.bfloat16)
    rows_first = lax.all_gather(delta_first, "in", axis=1, tiled=True).reshape(frames, rows, BLK)
    grad_first = jnp.einsum(
        "frkb,fro->rkbo", panels_first, rows_first, preferred_element_type=jnp.float32
    )
    grad_first = (grad_first * live_first.astype(jnp.float32)[:, :, None, None]).astype(
        jnp.bfloat16
    )
    return (estimate, grad_first, grad_second)


def solution(mesh):
    return jax.shard_map(
        shards,
        mesh=mesh,
        in_specs=(
            P("out", "in"),
            P(None, "in"),
            P("out", "in"),
            P("out", "in", None, None),
            P(("out", "in")),
            P("out", "in"),
            P("out", "in"),
            P("out", "in", None, None),
            P(("out", "in")),
            P(None, ("out", "in")),
        ),
        out_specs=(P(None, ("out", "in")), P("out", "in", None, None), P("out", "in", None, None)),
        check_vma=False,
    )
```

profile of v0, /device:TPU:0, one launch (start us, length us, event | category | flops | bytes accessed | tf_op | source)
XLA Modules:
  0.0 443.3 jit_solution(16326143040761354913)
XLA Ops:
  9.7 111.5 %all-gather.3.cloned.1.call-done = bf16[128,81920]{1,0:T(8,128)(2,1)} async-done(((bf16[8,81920]{1,0:T(8,128)(2,1)}), bf16[128,81920]{1,0:T(8,128)(2,1)}) %all-gather.3.cloned.1.call-update) | async-done | bytes 20971536 | tf_op jit(solution)/shard_map/all_gather | solution.py:28
  121.2 27.9 %copy.68 = bf16[128,81920]{0,1:T(8,128)(2,1)} copy(bf16[128,81920]{1,0:T(8,128)(2,1)} %all-gather.3.cloned.1.call-done) | data formatting | bytes 41943040 | tf_op jit(solution)/shard_map/all_gather | solution.py:28
  149.0 28.0 %copy.70 = bf16[128,320,256]{2,0,1:T(8,128)(2,1)} copy(bf16[128,320,256]{0,2,1:T(8,128)(2,1)} %bitcast.50) | data formatting | bytes 41943040 | tf_op jit(solution)/shard_map/reshape | solution.py:30
  177.0 9.8 %gather_fusion = bf16[64,128,256]{2,1,0:T(8,128)(2,1)} fusion(bf16[128,320,256]{2,0,1:T(8,128)(2,1)} %copy.70, s32[1024]{0:T(1024)S(1)} %pad_clamp_fusion.1), kind=kCustom, calls=%fused_computation | custom fusion | bytes 8388864 | tf_op jit(solution)/shard_map/jit(_take)/gather | solution.py:32
  186.8 6.5 %copy.71 = bf16[128,8,8,256]{0,3,2,1:T(8,128)(2,1)} copy(bf16[128,8,8,256]{3,0,2,1:T(8,128)(2,1)} %bitcast.53) | data formatting | bytes 8388608 | tf_op jit(solution)/shard_map/jit(_take)/gather | solution.py:32
  193.3 8.6 %fusion = f32[8,256,128,1]{2,1,3,0:T(8,128)} fusion(bf16[8,8,256,256]{3,2,1,0:T(8,128)(2,1)} %param.13, bf16[8,8]{1,0:T(8,128)(2,1)S(1)} %get-tuple-element.19, bf16[128,8,8,256]{0,3,2,1:T(8,128)(2,1)} %copy.71, pred[8,8]{1,0:T(8,128)(4,1)S(1)} %copy.67), kind=kOutput, calls=%fused_computation.4 | convolution fusion | flops 1080033280 | bytes 13631680 | tf_op jit(solution)/shard_map/frkb,rkbo->fro/dot_general | solution.py:35
  201.9 20.4 %reduce-scatter.4.cloned.1.call-done = f32[128,1024]{0,1:T(8,128)} async-done(((f32[128,2048]{0,1:T(8,128)}), f32[128,1024]{0,1:T(8,128)}) %reduce-scatter.4.cloned.1.call-update) | async-done | bytes 524304 | tf_op jit(solution)/shard_map/reduce_scatter | solution.py:38
  222.3 2.0 tanh_convert_fusion.1
  224.7 51.2 %all-gather.5.cloned.1.call-done = bf16[128,16384]{0,1:T(8,128)(2,1)} async-done(((bf16[128,1024]{0,1:T(8,128)(2,1)}), bf16[128,16384]{0,1:T(8,128)(2,1)}) %all-gather.5.cloned.1.call-update) | async-done | bytes 4194320 | tf_op jit(solution)/shard_map/all_gather | solution.py:40
  275.9 6.4 %copy.75 = bf16[128,64,256]{2,0,1:T(8,128)(2,1)} copy(bf16[128,64,256]{0,2,1:T(8,128)(2,1)} %bitcast.55) | data formatting | bytes 8388608 | tf_op jit(solution)/shard_map/reshape | solution.py:41
  282.3 2.9 gather_fusion.1
  285.1 2.4 copy.76
  287.6 5.5 %fusion.5 = f32[8,256,128,1]{2,1,3,0:T(8,128)} fusion(bf16[8,4,256,256]{3,2,1,0:T(8,128)(2,1)} %param.17, bf16[8,4]{1,0:T(8,128)(2,1)S(1)} %get-tuple-element.17, bf16[128,8,4,256]{0,3,2,1:T(8,128)(2,1)} %copy.76, pred[8,4]{1,0:T(8,128)(4,1)S(1)} %copy.66), kind=kOutput, calls=%fused_computation.11 | convolution fusion | flops 540016640 | bytes 7340128 | tf_op jit(solution)/shard_map/frkb,rkbo->fro/dot_general | solution.py:45
  293.3 18.6 %reduce-scatter.6.cloned.1.call-done = f32[128,1024]{0,1:T(8,128)} async-done(((f32[128,2048]{0,1:T(8,128)}), f32[128,1024]{0,1:T(8,128)}) %reduce-scatter.6.cloned.1.call-update) | async-done | bytes 524304 | tf_op jit(solution)/shard_map/reduce_scatter | solution.py:48
  312.0 1.2 multiply_convert_fusion.3
  313.3 8.9 %all_gather.14 = bf16[128,2048]{0,1:T(8,128)(2,1)S(1)} all-gather(bf16[128,1024]{0,1:T(8,128)(2,1)S(1)} %get-tuple-element.12), channel_id=1, replica_groups=mesh['out'=16,'in'=2] {'in'}, dimensions={1}, use_global_device_ids=true | all-gather | bytes 786432 | tf_op jit(solution)/shard_map/all_gather | solution.py:52
  322.2 5.5 %fusion.3 = f32[8,4,256,128]{3,2,1,0:T(8,128)} fusion(bf16[128,8,256,1]{0,2,3,1:T(8,128)(2,1)S(1)} %bitcast.56, bf16[8,4,256,256]{3,2,1,0:T(8,128)(2,1)} %param.17, bf16[8,4]{1,0:T(8,128)(2,1)S(1)} %get-tuple-element.17), kind=kOutput, calls=%fused_computation.9 | convolution fusion | flops 538968064 | bytes 8912960 | tf_op jit(solution)/shard_map/fro,rkbo->frkb/dot_general | solution.py:59
  327.7 5.4 %copy.82 = f32[128,32,256]{2,1,0:T(8,128)} copy(f32[128,32,256]{0,2,1:T(8,128)} %bitcast.51) | data formatting | bytes 8388608 | tf_op jit(solution)/shard_map/reshape | solution.py:61
  333.1 7.8 %convert_bitcast_fusion = bf16[128,64,256]{2,1,0:T(8,128)(2,1)} fusion(f32[128,32,256]{2,1,0:T(8,128)} %copy.82, s32[32]{0:T(128)S(1)} %reshape.208), kind=kOutput, calls=%fused_computation.6 | convolution fusion | flops 807405568 | bytes 8388736 | tf_op jit(solution)/shard_map/fjb,jc->fcb/dot_general | solution.py:66
  340.9 6.8 %copy.98 = bf16[128,64,256]{0,2,1:T(8,128)(2,1)} copy(bf16[128,64,256]{2,1,0:T(8,128)(2,1)} %convert_bitcast_fusion) | data formatting | bytes 8388608 | tf_op jit(solution)/shard_map/convert_element_type | solution.py:70
  349.5 3.3 multiply_convert_fusion.1
  352.8 67.8 %reduce-scatter.8.cloned.1.call-done = bf16[128,1024]{0,1:T(8,128)(2,1)} async-done(((bf16[128,16384]{0,1:T(8,128)(2,1)}), bf16[128,1024]{0,1:T(8,128)(2,1)}) %reduce-scatter.8.cloned.1.call-update) | async-done | bytes 262160 | tf_op jit(solution)/shard_map/reduce_scatter | solution.py:69
  421.8 7.0 %all_gather.15 = bf16[128,2048]{0,1:T(8,128)(2,1)S(1)} all-gather(bf16[128,1024]{0,1:T(8,128)(2,1)S(1)} %multiply_convert_fusion.2), channel_id=1, replica_groups=mesh['out'=16,'in'=2] {'in'}, dimensions={1}, use_global_device_ids=true | all-gather | bytes 786432 | tf_op jit(solution)/shard_map/all_gather | solution.py:74
  428.8 8.0 %multiply_convert_fusion = bf16[8,8,256,256]{3,2,1,0:T(8,128)(2,1)} fusion(bf16[128,8,256,1]{0,2,3,1:T(8,128)(2,1)S(1)} %bitcast.60, f32[8,8]{1,0:T(8,128)S(1)} %get-tuple-element.18, bf16[128,8,8,256]{0,3,2,1:T(8,128)(2,1)} %copy.71, pred[8,8]{1,0:T(8,128)(4,1)S(1)} %copy.67), kind=kOutput, calls=%fused_computation.2 | convolution fusion | flops 1084227584 | bytes 13107520 | tf_op jit(solution)/shard_map/frkb,fro->rkbo/dot_general | solution.py:75
  (42 shorter events, 6.1 us)
Async XLA Ops:
  7.2 114.0 %all-gather.3.cloned.1.call-start = ((), (), s32[]{:S(2)}) async-start(), calls=%async_computation.3 | async-start | bytes 22282240 | tf_op jit(solution)/shard_map/all_gather | solution.py:28
  7.9 214.4 %reduce-scatter.4.cloned.1.call-start = ((), (), s32[]{:S(2)}) async-start(), calls=%async_computation.4 | async-start | bytes 1572864 | tf_op jit(solution)/shard_map/reduce_scatter | solution.py:38
  193.3 29.0 %copy-start.3 = (f32[1024]{0:T(1024)S(1)}, f32[1024]{0:T(1024)}, u32[]{:S(2)}) copy-start(f32[1024]{0:T(1024)} %param.14) | copy-start | bytes 12292
  193.3 31.1 %copy-start.4 = (s32[8,4]{0,1:T(4,128)S(1)}, s32[8,4]{0,1:T(4,128)}, u32[]{:S(2)}) copy-start(s32[8,4]{0,1:T(4,128)} %param.15) | copy-start | bytes 388
  193.3 31.4 %copy-start.6 = (s32[8,1]{0,1:T(1,128)S(1)}, s32[8,1]{0,1:T(1,128)}, u32[]{:S(2)}) copy-start(s32[8,1]{0,1:T(1,128)} %param.16) | copy-start | bytes 100
  201.9 74.0 %all-gather.5.cloned.1.call-start = ((), (), s32[]{:S(2)}) async-start(), calls=%async_computation.5 | async-start | bytes 4456448 | tf_op jit(solution)/shard_map/all_gather | solution.py:40
  224.3 87.7 %reduce-scatter.6.cloned.1.call-start = ((), (), s32[]{:S(2)}) async-start(), calls=%async_computation.6 | async-start | bytes 1572864 | tf_op jit(solution)/shard_map/reduce_scatter | solution.py:48
  287.5 5.6 %copy-start.2 = (bf16[128,1024]{1,0:T(8,128)(2,1)S(1)}, bf16[128,1024]{1,0:T(8,128)(2,1)}, u32[]{:S(2)}) copy-start(bf16[128,1024]{1,0:T(8,128)(2,1)} %param.19) | copy-start | bytes 786436
  287.5 24.4 %copy-start.5 = (f32[1024]{0:T(1024)S(1)}, f32[1024]{0:T(1024)}, u32[]{:S(2)}) copy-start(f32[1024]{0:T(1024)} %param.18) | copy-start | bytes 12292
  293.0 127.6 %reduce-scatter.8.cloned.1.call-start = ((), (), s32[]{:S(2)}) async-start(), calls=%async_computation.7 | async-start | bytes 4456448 | tf_op jit(solution)/shard_map/reduce_scatter | solution.py:69
  347.8 1.7 copy-start
  347.8 72.8 %copy-start.1 = (f32[128,1024]{0,1:T(8,128)S(1)}, f32[128,1024]{0,1:T(8,128)}, u32[]{:S(2)}) copy-start(f32[128,1024]{0,1:T(8,128)} %reduce-scatter.4.cloned.1.call-done) | copy-start | bytes 1572868
Sparse Core Ops, SparseCore 0:
  9.6 111.5 all-gather.2
  202.0 20.2 reduce-scatter.3
  225.3 50.5 all-gather.4
  293.2 18.7 reduce-scatter.5
  347.9 72.6 reduce-scatter.7
where the time goes:
time: 446 us; the launch traced here: 443 us
  waiting for transfers between devices  270 us (61%)
  local copies, waits for them, and re-layouts  98.4 us (22%)
  matrix products  38.7 us (9%)
  blocking collectives  15.9 us (4%)
  between operations  13.9 us (3%)
  other arithmetic  5.97 us (1%)
    all_gather x1, waiting for transfers between devices, shards(): gathered = lax.all_gather(slopes, 'out', axis=0, tiled=True)  111 us
    reduce_scatter x1, waiting for transfers between devices, shards(): lax.psum_scatter(spread.astype(jnp.bfloat16), 'out', scatter_dimension=1,...  67.8 us
    all_gather x1, waiting for transfers between devices, shards(): second_input = lax.all_gather(hidden_first, 'out', axis=1, tiled=True)  51.2 us
    reshape x1, local copies, waits for them, and re-layouts, shards(): slope_blocks = gathered.reshape(frames, -1, BLK)  28 us
    all_gather x1, local copies, waits for them, and re-layouts, shards(): gathered = lax.all_gather(slopes, 'out', axis=0, tiled=True)  27.9 us
    reduce_scatter x1, waiting for transfers between devices, shards(): lax.psum_scatter(partial_first, 'in', scatter_dimension=1, tiled=True)  20.4 us
    reduce_scatter x1, waiting for transfers between devices, shards(): lax.psum_scatter(partial_second, 'in', scatter_dimension=1, tiled=True)  18.6 us
    gather x2, local copies, waits for them, and re-layouts, shards(): jnp.take(slope_blocks, own_cols.reshape(-1), axis=1)  16.3 us
  transfers between devices with their start and end apart: 5, of which 5 were waited for; matrix products, arithmetic and copies ran while one was open for 1% of the time, Pallas kernels for 0%

commit v1 on v0

v1 whole, which is shorter than its diff:
```python
import functools

import jax
import jax.numpy as jnp
from jax import lax
from jax.experimental import pallas as pl
from jax.experimental.pallas import tpu as pltpu
from jax.sharding import PartitionSpec as P

BLK = 256
KD1 = 8
KD2 = 4
VMEM_LIMIT = 48 * 1024 * 1024
F32 = jnp.float32
BF16 = jnp.bfloat16


def params():
    return pltpu.CompilerParams(vmem_limit_bytes=VMEM_LIMIT)


def panel_block(frames, sub):
    return (1, frames, BLK) if sub >= BLK else (BLK // sub, frames, sub)


def panel_place(sub, block):
    if sub >= BLK:
        per = sub // BLK
        return (block // per, 0, block % per)
    return (block, 0, 0)


def read_panel(ref):
    if len(ref.shape) == 2:
        return ref[...]
    parts = [ref[i] for i in range(ref.shape[0])]
    return parts[0] if len(parts) == 1 else jnp.concatenate(parts, axis=1)


def write_panel(ref, value):
    width = ref.shape[2]
    for i in range(ref.shape[0]):
        ref[i] = value[:, i * width : (i + 1) * width].astype(ref.dtype)


def forward_kernel(slots, cols, counts, *refs):
    panels, weight, out = refs[:slots], refs[slots], refs[slots + 1]
    live = counts[pl.program_id(0)]
    total = None
    for k in range(slots):
        term = jnp.dot(read_panel(panels[k]), weight[0, k], preferred_element_type=F32)
        term = jnp.where(k < live, term, 0.0)
        total = term if total is None else total + term
    write_panel(out, total)


def grad_kernel(slots, cols, counts, *refs):
    panels, delta, out = refs[:slots], refs[slots], refs[slots + 1]
    live = counts[pl.program_id(0)]
    rows = read_panel(delta)
    for k in range(slots):
        term = lax.dot_general(
            read_panel(panels[k]), rows, (((0,), (0,)), ((), ())), preferred_element_type=F32
        )
        out[0, k] = jnp.where(k < live, term, 0.0).astype(out.dtype)


def adjoint_kernel(slots, cols, counts, delta, weight, out, total):
    row = pl.program_id(0)
    live = counts[row]

    @pl.when(row == 0)
    def _():
        total[...] = jnp.zeros_like(total)

    rows = read_panel(delta)
    for k in range(slots):
        term = lax.dot_general(
            rows, weight[0, k], (((1,), (1,)), ((), ())), preferred_element_type=F32
        )
        place = cols[row * slots + k]
        total[place] += jnp.where(k < live, term, 0.0)

    @pl.when(row == pl.num_programs(0) - 1)
    def _():
        pieces, frames, sub = out.shape
        if sub >= BLK:
            per = sub // BLK
            for c in range(total.shape[0]):
                at = (c % per) * BLK
                out[c // per, :, at : at + BLK] = total[c].astype(out.dtype)
        else:
            per = BLK // sub
            for p in range(pieces):
                at = (p % per) * sub
                out[p] = total[p // per, :, at : at + sub].astype(out.dtype)


def panel_specs(slots, frames, sub):
    def spec(k):
        if sub is None:
            return pl.BlockSpec((frames, BLK), lambda r, cols, counts: (0, cols[r * slots + k]))
        return pl.BlockSpec(
            panel_block(frames, sub),
            lambda r, cols, counts: panel_place(sub, cols[r * slots + k]),
        )

    return [spec(k) for k in range(slots)]


def row_spec(frames, sub):
    return pl.BlockSpec(panel_block(frames, sub), lambda r, cols, counts: panel_place(sub, r))


def weight_spec(slots):
    return pl.BlockSpec((1, slots, BLK, BLK), lambda r, cols, counts: (r, 0, 0, 0))


def forward(inputs, in_sub, cols, counts, weight, frames, pieces, sub):
    rows, slots = weight.shape[:2]
    return pl.pallas_call(
        functools.partial(forward_kernel, slots),
        grid_spec=pltpu.PrefetchScalarGridSpec(
            num_scalar_prefetch=2,
            grid=(rows,),
            in_specs=panel_specs(slots, frames, in_sub) + [weight_spec(slots)],
            out_specs=row_spec(frames, sub),
        ),
        out_shape=jax.ShapeDtypeStruct((pieces, frames, sub), F32),
        compiler_params=params(),
    )(cols, counts, *([inputs] * slots), weight)


def weight_grad(inputs, in_sub, cols, counts, delta, slots):
    pieces, frames, sub = delta.shape
    rows = pieces * sub // BLK
    return pl.pallas_call(
        functools.partial(grad_kernel, slots),
        grid_spec=pltpu.PrefetchScalarGridSpec(
            num_scalar_prefetch=2,
            grid=(rows,),
            in_specs=panel_specs(slots, frames, in_sub) + [row_spec(frames, sub)],
            out_specs=weight_spec(slots),
        ),
        out_shape=jax.ShapeDtypeStruct((rows, slots, BLK, BLK), BF16),
        cost_estimate=pl.CostEstimate(
            flops=2 * rows * slots * frames * BLK * BLK,
            bytes_accessed=2 * rows * slots * BLK * (BLK + frames),
            transcendentals=0,
        ),
        compiler_params=params(),
    )(cols, counts, *([inputs] * slots), delta)


def adjoint(delta, weight, cols, counts, out_pieces):
    pieces, frames, sub = delta.shape
    rows, slots = weight.shape[:2]
    return pl.pallas_call(
        functools.partial(adjoint_kernel, slots),
        grid_spec=pltpu.PrefetchScalarGridSpec(
            num_scalar_prefetch=2,
            grid=(rows,),
            in_specs=[row_spec(frames, sub), weight_spec(slots)],
            out_specs=pl.BlockSpec((out_pieces, frames, sub), lambda r, cols, counts: (0, 0, 0)),
            scratch_shapes=[pltpu.VMEM((out_pieces * sub // BLK, frames, BLK), F32)],
        ),
        out_shape=jax.ShapeDtypeStruct((out_pieces, frames, sub), BF16),
        compiler_params=params(),
    )(cols, counts, delta, weight)


def shards(
    n_out,
    n_in,
    slopes,
    cols_first,
    count_first,
    weight_first,
    bias_first,
    cols_second,
    count_second,
    weight_second,
    bias_second,
    cotangent,
):
    rows = weight_first.shape[0]
    frames = slopes.shape[0] * n_out
    sub = bias_first.shape[0]
    first = lax.dynamic_slice_in_dim(cols_first, lax.axis_index("out") * rows, rows, 0).reshape(-1)
    second = cols_second.reshape(-1)
    live_first, live_second = count_first.reshape(-1), count_second.reshape(-1)

    gathered = lax.all_gather(slopes, "out", axis=0, tiled=True)
    partial_first = forward(gathered, None, first, live_first, weight_first, frames, n_in, sub)
    summed_first = lax.psum_scatter(partial_first, "in", scatter_dimension=0, tiled=False)
    hidden = jnp.tanh(summed_first + bias_first[None, :]).astype(BF16)

    ordered = lax.all_gather(hidden, "out", axis=0, tiled=False)
    partial_second = forward(ordered, sub, second, live_second, weight_second, frames, n_in, sub)
    summed_second = lax.psum_scatter(partial_second, "in", scatter_dimension=0, tiled=False)
    estimate = jnp.tanh(summed_second + bias_second[None, :]).astype(BF16)
    est32 = estimate.astype(F32)
    delta_second = (cotangent.astype(F32) * (1.0 - est32 * est32)).astype(BF16)

    rows_second = lax.all_gather(delta_second, "in", axis=0, tiled=False)
    spread = adjoint(rows_second, weight_second, second, live_second, n_out)
    back = lax.psum_scatter(spread, "out", scatter_dimension=0, tiled=False).astype(F32)
    grad_second = weight_grad(ordered, sub, second, live_second, rows_second, KD2)
    hid32 = hidden.astype(F32)
    delta_first = (back * (1.0 - hid32 * hid32)).astype(BF16)
    rows_first = lax.all_gather(delta_first, "in", axis=0, tiled=False)
    grad_first = weight_grad(gathered, None, first, live_first, rows_first, KD1)
    return (estimate, grad_first, grad_second)


def solution(mesh):
    return jax.shard_map(
        functools.partial(shards, mesh.shape["out"], mesh.shape["in"]),
        mesh=mesh,
        in_specs=(
            P("out", "in"),
            P(None, "in"),
            P("out", "in"),
            P("out", "in", None, None),
            P(("out", "in")),
            P("out", "in"),
            P("out", "in"),
            P("out", "in", None, None),
            P(("out", "in")),
            P(None, ("out", "in")),
        ),
        out_specs=(P(None, ("out", "in")), P("out", "in", None, None), P("out", "in", None, None)),
        check_vma=False,
    )
```

time: 446 us -> 352 us (0.79)
  local copies, waits for them, and re-layouts: 98.4 us -> 7.46 us
  Pallas kernels: 0 us -> 40.3 us
  matrix products: 38.7 us -> 0 us
    pallas_call x0 -> x5, Pallas kernels: none -> 40.3 us  [the longest x2 17 us: forward(): pl.pallas_call(functools.partial(forward_kernel, slots), grid_spec=pltpu....]
    reshape x6 -> x2, local copies, waits for them, and re-layouts: 40 us -> 0.16 us  [the longest x1 0.08 us: shards(): lax.dynamic_slice_in_dim(cols_first, lax.axis_index('out') * rows, rows, 0)]
    dot_general x6 -> x0, matrix products: 38.7 us -> none  [the longest x1 8.57 us: shards(): jnp.einsum('frkb,rkbo->fro', panels_first, masked_first, preferred_elemen...]
    all_gather x1 -> x0, local copies, waits for them, and re-layouts: 27.9 us -> none  [shards(): gathered = lax.all_gather(slopes, 'out', axis=0, tiled=True)]
    gather x4 -> x0, local copies, waits for them, and re-layouts: 21.5 us -> none  [the longest x2 16.3 us: shards(): jnp.take(slope_blocks, own_cols.reshape(-1), axis=1)]
    convert_element_type x1 -> x0, local copies, waits for them, and re-layouts: 6.82 us -> none  [shards(): spread.astype(jnp.bfloat16)]
    unnamed x17 -> x25, local copies, waits for them, and re-layouts: 1.93 us -> 7.15 us
  transfers between devices with their start and end apart: 5 -> 5, of which waited for: 5 -> 5; matrix products, arithmetic and copies ran while one was open for 1% -> 0% of each run, Pallas kernels for 0% -> 2%
where the time goes in v1:
time: 352 us; the launch traced here: 351 us
  waiting for transfers between devices  269 us (76%)
  Pallas kernels  40.3 us (11%)
  blocking collectives  15.8 us (4%)
  between operations  13.8 us (4%)
  local copies, waits for them, and re-layouts  7.46 us (2%)
  other arithmetic  4.78 us (1%)
    all_gather x1, waiting for transfers between devices, shards(): gathered = lax.all_gather(slopes, 'out', axis=0, tiled=True)  113 us
    reduce_scatter x1, waiting for transfers between devices, shards(): lax.psum_scatter(spread, 'out', scatter_dimension=0, tiled=False)  64.5 us
    all_gather x1, waiting for transfers between devices, shards(): ordered = lax.all_gather(hidden, 'out', axis=0, tiled=False)  51.5 us
    reduce_scatter x1, waiting for transfers between devices, shards(): lax.psum_scatter(partial_first, 'in', scatter_dimension=0, tiled=False)  20.4 us
    reduce_scatter x1, waiting for transfers between devices, shards(): lax.psum_scatter(partial_second, 'in', scatter_dimension=0, tiled=False)  18.9 us
    pallas_call x2, Pallas kernels, forward(): pl.pallas_call(functools.partial(forward_kernel, slots), grid_spec=pltpu....  17 us
    pallas_call x2, Pallas kernels, weight_grad(): pl.pallas_call(functools.partial(grad_kernel, slots), grid_spec=pltpu.Pre...  15.6 us
    all_gather x1, blocking collectives, shards(): rows_second = lax.all_gather(delta_second, 'in', axis=0, tiled=False)  8.71 us
  transfers between devices with their start and end apart: 5, of which 5 were waited for; matrix products, arithmetic and copies ran while one was open for 0% of the time, Pallas kernels for 2%

profile of v1, /device:TPU:0, one launch (start us, length us, event | category | flops | bytes accessed | tf_op | source)
XLA Modules:
  0.0 351.4 jit_solution(18013735523903768875)
XLA Ops:
  7.2 0.7 all-gather.4.cloned.1.call-update
  8.0 0.1 constant_dynamic-slice_fusion
  8.1 0.1 reshape.33.cols
  8.2 113.0 %all-gather.4.cloned.1.call-done.refs_0_.refs_1_.refs_2_.refs_3_.refs_4_.refs_5_.refs_6_.refs_7_ = bf16[128,81920]{1,0:T(8,128)(2,1)} async-done(((bf16[8,81920]{1,0:T(8,128)(2,1)}), bf16[128,81920]{1,0:T(8,128)(2,1)}) %all-gather.4.cloned.1.call-update) | async-done | bytes 20971536 | tf_op jit(solution)/shard_map/all_gather | solution.py:193
  121.2 0.7 copy-done.5
  121.8 9.3 %shard_map.121 = f32[2,128,1024]{2,1,0:T(8,128)} custom-call(s32[64]{0:T(128)S(1)} %reshape.33.cols, s32[8]{0:T(128)S(1)} %bitcast.15, bf16[128,81920]{1,0:T(8,128)(2,1)} %all-gather.4.cloned.1.call-done.refs_0_.refs_1_.refs_2_.refs_3_.refs_4_.refs_5_.refs_6_.refs_7_, ...), custom_call_target="tpu_custom_call" | custom-call | tf_op jit(solution)/shard_map/pallas_call | solution.py:121
  131.2 20.4 %reduce-scatter.4.cloned.1.call-done = f32[1,128,1024]{2,1,0:T(8,128)} async-done(((f32[2,128,1024]{2,1,0:T(8,128)}), f32[1,128,1024]{2,1,0:T(8,128)}) %reduce-scatter.4.cloned.1.call-update) | async-done | bytes 524304 | tf_op jit(solution)/shard_map/reduce_scatter | solution.py:195
  151.6 1.8 tanh_convert_fusion
  153.5 0.1 copy.17
  153.6 0.1 reshape.31.cols
  153.7 51.5 %all-gather.6.cloned.1.call-done.refs_0_.refs_1_.refs_2_.refs_3_ = bf16[16,128,1024]{2,1,0:T(8,128)(2,1)} async-done(((bf16[1,128,1024]{2,1,0:T(8,128)(2,1)}), bf16[16,128,1024]{2,1,0:T(8,128)(2,1)}) %all-gather.6.cloned.1.call-update) | async-done | bytes 4194320 | tf_op jit(solution)/shard_map/all_gather | solution.py:198
  205.2 2.2 copy-done.1
  207.4 7.6 %shard_map.122 = f32[2,128,1024]{2,1,0:T(8,128)} custom-call(s32[32]{0:T(128)S(1)} %reshape.31.cols, s32[8]{0:T(128)S(1)} %bitcast.12, bf16[16,128,1024]{2,1,0:T(8,128)(2,1)S(1)} %copy-done.1, bf16[16,128,1024]{2,1,0:T(8,128)(2,1)S(1)} %copy-done.1, bf16[16,128,1024]{2,1,0:T(8,128)(2,1)S(1)} %copy-done.1, bf16[16,128,1024]{2,1,0:T(8,128)(2,1)S(1)} %copy-done.1, ...), custom_call_target="tpu_custom_call" | custom-call | tf_op jit(solution)/shard_map/pallas_call | solution.py:121
  215.1 18.9 %reduce-scatter.6.cloned.1.call-done = f32[1,128,1024]{2,1,0:T(8,128)} async-done(((f32[2,128,1024]{2,1,0:T(8,128)}), f32[1,128,1024]{2,1,0:T(8,128)}) %reduce-scatter.6.cloned.1.call-update) | async-done | bytes 524304 | tf_op jit(solution)/shard_map/reduce_scatter | solution.py:200
  234.1 1.9 multiply_convert_fusion.1
  235.9 8.7 %all-gather = bf16[256,1024]{1,0:T(8,128)(2,1)S(1)} all-gather(bf16[128,1024]{1,0:T(8,128)(2,1)S(1)} %get-tuple-element.3), channel_id=2, replica_groups=mesh['out'=16,'in'=2] {'in'}, dimensions={0}, use_global_device_ids=true | all-gather | bytes 786432 | tf_op jit(solution)/shard_map/all_gather | solution.py:205
  244.7 7.7 %shard_map.123 = bf16[16,128,1024]{2,1,0:T(8,128)(2,1)S(1)} custom-call(s32[32]{0:T(128)S(1)} %reshape.31.cols, s32[8]{0:T(128)S(1)} %bitcast.13, bf16[2,128,1024]{2,1,0:T(8,128)(2,1)S(1)} %bitcast.10, bf16[8,4,256,256]{3,2,1,0:T(8,128)(2,1)} %weight.1), custom_call_target="tpu_custom_call" | custom-call | tf_op jit(solution)/shard_map/pallas_call | solution.py:158
  252.4 2.0 copy-done.3
  254.4 2.2 copy-done.2
  256.6 6.1 %shard_map.125 = bf16[8,4,256,256]{3,2,1,0:T(8,128)(2,1)} custom-call(s32[32]{0:T(128)S(1)} %reshape.31.cols, s32[8]{0:T(128)S(1)} %bitcast.14, bf16[16,128,1024]{2,1,0:T(8,128)(2,1)S(1)} %copy-done.2, bf16[16,128,1024]{2,1,0:T(8,128)(2,1)S(1)} %copy-done.2, bf16[16,128,1024]{2,1,0:T(8,128)(2,1)S(1)} %copy-done.2, bf16[16,128,1024]{2,1,0:T(8,128)(2,1)S(1)} %copy-done.2, ...), custom_call_target="tpu_custom_call" | custom-call | flops 536870912 | bytes 6291456 | tf_op jit(solution)/shard_map/pallas_call | solution.py:137
  262.7 64.5 %reduce-scatter.8.cloned.1.call-done = bf16[1,128,1024]{2,1,0:T(8,128)(2,1)} async-done(((bf16[16,128,1024]{2,1,0:T(8,128)(2,1)}), bf16[1,128,1024]{2,1,0:T(8,128)(2,1)}) %reduce-scatter.8.cloned.1.call-update) | async-done | bytes 262160 | tf_op jit(solution)/shard_map/reduce_scatter | solution.py:207
  327.3 1.1 multiply_convert_fusion
  328.3 7.0 %all_gather.21.refs_8_ = bf16[2,128,1024]{2,1,0:T(8,128)(2,1)S(1)} all-gather(bf16[1,128,1024]{2,1,0:T(8,128)(2,1)S(1)} %multiply_convert_fusion), channel_id=1, replica_groups=mesh['out'=16,'in'=2] {'in'}, dimensions={0}, use_global_device_ids=true | all-gather | bytes 786432 | tf_op jit(solution)/shard_map/all_gather | solution.py:211
  335.4 9.5 %shard_map.124 = bf16[8,8,256,256]{3,2,1,0:T(8,128)(2,1)} custom-call(s32[64]{0:T(128)S(1)} %reshape.33.cols, s32[8]{0:T(128)S(1)} %bitcast.16, bf16[128,81920]{1,0:T(8,128)(2,1)} %all-gather.4.cloned.1.call-done.refs_0_.refs_1_.refs_2_.refs_3_.refs_4_.refs_5_.refs_6_.refs_7_, ...), custom_call_target="tpu_custom_call" | custom-call | flops 1073741824 | bytes 12582912 | tf_op jit(solution)/shard_map/pallas_call | solution.py:137
  (30 shorter events, 0.4 us)
Async XLA Ops:
  7.2 0.8 copy-start
  7.2 114.0 %all-gather.4.cloned.1.call-start = ((), (), s32[]{:S(2)}) async-start(), calls=%async_computation.3 | async-start | bytes 22282240 | tf_op jit(solution)/shard_map/all_gather | solution.py:193
  7.9 143.7 %reduce-scatter.4.cloned.1.call-start = ((), (), s32[]{:S(2)}) async-start(), calls=%async_computation.4 | async-start | bytes 1572864 | tf_op jit(solution)/shard_map/reduce_scatter | solution.py:195
  121.2 0.7 copy-start.5
  121.8 29.8 %copy-start.9 = (f32[1024]{0:T(1024)S(1)}, f32[1024]{0:T(1024)}, u32[]{:S(2)}) copy-start(f32[1024]{0:T(1024)} %param.14) | copy-start | bytes 12292
  121.8 31.7 %copy-start.11 = (s32[8,4]{0,1:T(4,128)S(1)}, s32[8,4]{0,1:T(4,128)}, u32[]{:S(2)}) copy-start(s32[8,4]{0,1:T(4,128)} %param.15) | copy-start | bytes 388
  121.8 83.4 %copy-start.4 = (s32[8,1]{0,1:T(1,128)S(1)}, s32[8,1]{0,1:T(1,128)}, u32[]{:S(2)}) copy-start(s32[8,1]{0,1:T(1,128)} %param.16) | copy-start | bytes 100
  131.2 74.0 %all-gather.6.cloned.1.call-start = ((), (), s32[]{:S(2)}) async-start(), calls=%async_computation.5 | async-start | bytes 4456448 | tf_op jit(solution)/shard_map/all_gather | solution.py:198
  153.5 80.6 %reduce-scatter.6.cloned.1.call-start = ((), (), s32[]{:S(2)}) async-start(), calls=%async_computation.6 | async-start | bytes 1572864 | tf_op jit(solution)/shard_map/reduce_scatter | solution.py:200
  205.2 2.2 copy-start.1
  207.4 26.7 %copy-start.8 = (bf16[128,1024]{1,0:T(8,128)(2,1)S(1)}, bf16[128,1024]{1,0:T(8,128)(2,1)}, u32[]{:S(2)}) copy-start(bf16[128,1024]{1,0:T(8,128)(2,1)} %param.19) | copy-start | bytes 786436
  207.4 26.7 %copy-start.10 = (f32[1024]{0:T(1024)S(1)}, f32[1024]{0:T(1024)}, u32[]{:S(2)}) copy-start(f32[1024]{0:T(1024)} %param.18) | copy-start | bytes 12292
  215.1 112.2 %reduce-scatter.8.cloned.1.call-start = ((), (), s32[]{:S(2)}) async-start(), calls=%async_computation.7 | async-start | bytes 4456448 | tf_op jit(solution)/shard_map/reduce_scatter | solution.py:207
  252.4 2.0 copy-start.3
  254.4 2.2 copy-start.2
  256.6 70.6 %copy-start.7 = (f32[1,128,1024]{2,1,0:T(8,128)S(1)}, f32[1,128,1024]{2,1,0:T(8,128)}, u32[]{:S(2)}) copy-start(f32[1,128,1024]{2,1,0:T(8,128)} %reduce-scatter.4.cloned.1.call-done) | copy-start | bytes 1572868
  256.6 78.8 %copy-start.6 = (s32[8,1]{0,1:T(1,128)S(1)}, s32[8,1]{0,1:T(1,128)}, u32[]{:S(2)}) copy-start(s32[8,1]{0,1:T(1,128)} %param.12) | copy-start | bytes 100
Sparse Core Ops, SparseCore 0:
  9.6 111.5 all-gather.3
  131.3 20.2 reduce-scatter.3
  154.6 50.5 all-gather.5
  215.2 18.8 reduce-scatter.5
  254.6 72.6 reduce-scatter.7

commit v2 on v1

--- a/solution.py
+++ b/solution.py
@@ -167,6 +167,313 @@
         out_shape=jax.ShapeDtypeStruct((out_pieces, frames, sub), BF16),
         compiler_params=params(),
     )(cols, counts, delta, weight)
+
+
+MESH = pl.DeviceIdType.MESH
+STEP = 16
+SIDE = 4
+
+
+def by_rows(frames, body):
+    def turn(i, carry):
+        body(pl.ds(pl.multiple_of(i * STEP, STEP), STEP))
+        return carry
+
+    lax.fori_loop(0, frames // STEP, turn, 0)
+
+
+def remote(source, target, send, recv, peer):
+    return pltpu.make_async_remote_copy(
+        src_ref=source,
+        dst_ref=target,
+        send_sem=send,
+        recv_sem=recv,
+        device_id=peer,
+        device_id_type=MESH,
+    )
+
+
+def greet(peers):
+    barrier = pltpu.get_barrier_semaphore()
+    for peer in peers:
+        pl.semaphore_signal(barrier, inc=1, device_id=peer, device_id_type=MESH)
+    pl.semaphore_wait(barrier, len(peers))
+
+
+def in_peers(n_in):
+    me = lax.axis_index("in")
+    return [{"in": lax.rem(me + t, n_in)} for t in range(1, n_in)]
+
+
+def out_place(n_out):
+    me = lax.axis_index("out")
+    inner = lax.rem(me, SIDE)
+    core = lax.rem(me, 2)
+    column = lax.rem(lax.div(me, 2), 2)
+    return me, lax.div(me, SIDE), inner, me + 1 - 2 * core, me + 2 - 4 * column
+
+
+def out_peers(n_out):
+    me, outer, inner, core_peer, x_peer = out_place(n_out)
+    count = n_out // SIDE
+    far = [{"out": lax.rem(outer + t, count) * SIDE + inner} for t in range(1, count)]
+    return [{"out": core_peer}, {"out": x_peer}] + far
+
+
+def exchange_start(n_in, partial, leaving, arriving, send, recv):
+    copies = []
+    for t, peer in enumerate(in_peers(n_in)):
+        def cast(at, t=t, peer=peer):
+            leaving[t, at, :] = partial[peer["in"], at, :].astype(BF16)
+
+        by_rows(partial.shape[1], cast)
+        copy = remote(leaving.at[t], arriving.at[t], send.at[t], recv.at[t], peer)
+        copy.start()
+        copies.append(copy)
+    for copy in copies:
+        copy.wait()
+
+
+def exchanged(n_in, partial, arriving, bias, at):
+    total = partial[lax.axis_index("in"), at, :]
+    for t in range(n_in - 1):
+        total = total + arriving[t, at, :].astype(F32)
+    return total + bias[...]
+
+
+def share_in(n_in, rows, send, recv):
+    me = lax.axis_index("in")
+    copies = []
+    for t, peer in enumerate(in_peers(n_in)):
+        copy = remote(rows.at[me], rows.at[me], send.at[t], recv.at[t], peer)
+        copy.start()
+        copies.append(copy)
+    for copy in copies:
+        copy.wait()
+
+
+def hidden_kernel(
+    n_out, n_in, partial, bias, hidden, ordered, leaving, arriving, in_send, in_recv, send, recv, own
+):
+    frames = hidden.shape[0]
+    greet(in_peers(n_in) + out_peers(n_out))
+    exchange_start(n_in, partial, leaving, arriving, in_send, in_recv)
+
+    def finish(at):
+        hidden[at, :] = jnp.tanh(exchanged(n_in, partial, arriving, bias, at)).astype(BF16)
+
+    by_rows(frames, finish)
+    me, outer, inner, core_peer, x_peer = out_place(n_out)
+    count = n_out // SIDE
+    copies = []
+
+    def forward_to(source, block, target):
+        k = len(copies)
+        copy = remote(source, ordered.at[block], send.at[k], recv.at[block], {"out": target})
+        copy.start()
+        copies.append(copy)
+
+    def arrived(block):
+        remote(hidden, ordered.at[block], send.at[0], recv.at[block], {"out": core_peer}).wait_recv()
+
+    def held(t, place):
+        return lax.rem(outer + t, count) * SIDE + place
+
+    for t in range(1, count):
+        forward_to(hidden, me, held(t, inner))
+    forward_to(hidden, me, x_peer)
+    forward_to(hidden, me, core_peer)
+    keep = pltpu.make_async_copy(hidden, ordered.at[me], own)
+    keep.start()
+    across = lax.rem(x_peer, SIDE)
+    for t in range(1, count + 1):
+        if t < count:
+            block = held(t, inner)
+            arrived(block)
+            forward_to(ordered.at[block], block, x_peer)
+            forward_to(ordered.at[block], block, core_peer)
+        block = held(t - 1, across)
+        arrived(block)
+        forward_to(ordered.at[block], block, core_peer)
+    for t in range(count):
+        for place in (lax.rem(core_peer, SIDE), SIDE - 1 - inner):
+            arrived(held(t, place))
+    for copy in copies:
+        copy.wait_send()
+    keep.wait()
+
+
+def estimate_kernel(
+    n_in, partial, bias, cotangent, estimate, rows, leaving, arriving, in_send, in_recv, send, recv
+):
+    greet(in_peers(n_in))
+    exchange_start(n_in, partial, leaving, arriving, in_send, in_recv)
+    me = lax.axis_index("in")
+
+    def finish(at):
+        value = jnp.tanh(exchanged(n_in, partial, arriving, bias, at)).astype(BF16)
+        estimate[at, :] = value
+        wide = value.astype(F32)
+        rows[me, at, :] = (cotangent[at, :].astype(F32) * (1.0 - wide * wide)).astype(BF16)
+
+    by_rows(estimate.shape[0], finish)
+    share_in(n_in, rows, send, recv)
+
+
+def reduce_kernel(
+    n_out, n_in, spread, hidden, rows,
+    from_core, to_x, from_x, to_z, from_z,
+    core_send, core_recv, x_send, x_recv, z_send, z_recv, in_send, in_recv,
+):
+    frames = hidden.shape[0]
+    count = n_out // SIDE
+    greet(in_peers(n_in) + out_peers(n_out))
+    me, outer, inner, core_peer, x_peer = out_place(n_out)
+    across = lax.rem(x_peer, SIDE)
+    core_inner, core_across = lax.rem(core_peer, SIDE), SIDE - 1 - inner
+
+    def held(t, place):
+        return lax.rem(outer + t, count) * SIDE + place
+
+    core_copies, x_copies, z_copies = [], [], []
+    for t in range(1, count + 1):
+        for place in (core_across, core_inner):
+            k = len(core_copies)
+            copy = remote(
+                spread.at[held(t, place)], from_core.at[k], core_send.at[k], core_recv.at[k],
+                {"out": core_peer},
+            )
+            copy.start()
+            core_copies.append(copy)
+
+    def column_sum(t, at):
+        total = spread[held(t, inner), at, :].astype(F32)
+        total = total + from_core[2 * t - 1, at, :].astype(F32)
+        return total + from_x[t - 1, at, :].astype(F32)
+
+    for t in range(1, count + 2):
+        if t <= count:
+            core_copies[2 * t - 2].wait_recv()
+
+            def add_core(at, t=t):
+                total = spread[held(t, across), at, :].astype(F32)
+                to_x[t - 1, at, :] = (total + from_core[2 * t - 2, at, :].astype(F32)).astype(BF16)
+
+            by_rows(frames, add_core)
+            copy = remote(
+                to_x.at[t - 1], from_x.at[t - 1], x_send.at[t - 1], x_recv.at[t - 1],
+                {"out": x_peer},
+            )
+            copy.start()
+            x_copies.append(copy)
+        s = t - 1
+        if s >= 1:
+            core_copies[2 * s - 1].wait_recv()
+            x_copies[s - 1].wait_recv()
+        if 1 <= s < count:
+
+            def add_x(at, s=s):
+                to_z[s - 1, at, :] = column_sum(s, at).astype(BF16)
+
+            by_rows(frames, add_x)
+            copy = remote(
+                to_z.at[s - 1], from_z.at[s - 1], z_send.at[s - 1], z_recv.at[s - 1],
+                {"out": held(s, inner)},
+            )
+            copy.start()
+            z_copies.append(copy)
+    for copy in z_copies:
+        copy.wait_recv()
+    place = lax.axis_index("in")
+
+    def finish(at):
+        total = column_sum(count, at)
+        for s in range(count - 1):
+            total = total + from_z[s, at, :].astype(F32)
+        wide = hidden[at, :].astype(F32)
+        rows[place, at, :] = (total * (1.0 - wide * wide)).astype(BF16)
+
+    by_rows(frames, finish)
+    share_in(n_in, rows, in_send, in_recv)
+    for copy in core_copies + x_copies + z_copies:
+        copy.wait_send()
+
+
+def whole_specs(count):
+    return [pl.BlockSpec(memory_space=pltpu.VMEM)] * count
+
+
+def dma(count):
+    return pltpu.SemaphoreType.DMA((count,))
+
+
+def remote_params(collective_id):
+    return pltpu.CompilerParams(
+        collective_id=collective_id, has_side_effects=True, vmem_limit_bytes=VMEM_LIMIT
+    )
+
+
+def hidden_layer(n_out, n_in, partial, bias):
+    _, frames, sub = partial.shape
+    return pl.pallas_call(
+        functools.partial(hidden_kernel, n_out, n_in),
+        out_shape=(
+            jax.ShapeDtypeStruct((frames, sub), BF16),
+            jax.ShapeDtypeStruct((n_out, frames, sub), BF16),
+        ),
+        in_specs=whole_specs(2),
+        out_specs=(pl.BlockSpec(memory_space=pltpu.VMEM), pl.BlockSpec(memory_space=pl.ANY)),
+        scratch_shapes=[
+            pltpu.VMEM((n_in - 1, frames, sub), BF16),
+            pltpu.VMEM((n_in - 1, frames, sub), BF16),
+            dma(n_in - 1),
+            dma(n_in - 1),
+            dma(n_out),
+            dma(n_out),
+            pltpu.SemaphoreType.DMA,
+        ],
+        compiler_params=remote_params(1),
+    )(partial, bias.reshape(1, -1))
+
+
+def estimate_layer(n_in, partial, bias, cotangent):
+    _, frames, sub = partial.shape
+    return pl.pallas_call(
+        functools.partial(estimate_kernel, n_in),
+        out_shape=(
+            jax.ShapeDtypeStruct((frames, sub), BF16),
+            jax.ShapeDtypeStruct((n_in, frames, sub), BF16),
+        ),
+        in_specs=whole_specs(3),
+        out_specs=tuple(whole_specs(2)),
+        scratch_shapes=[
+            pltpu.VMEM((n_in - 1, frames, sub), BF16),
+            pltpu.VMEM((n_in - 1, frames, sub), BF16),
+            dma(n_in - 1),
+            dma(n_in - 1),
+            dma(n_in - 1),
+            dma(n_in - 1),
+        ],
+        compiler_params=remote_params(2),
+    )(partial, bias.reshape(1, -1), cotangent)
+
+
+def reduce_layer(n_out, n_in, spread, hidden):
+    _, frames, sub = spread.shape
+    count = n_out // SIDE
+    blocks = lambda n: pltpu.VMEM((n, frames, sub), BF16)
+    return pl.pallas_call(
+        functools.partial(reduce_kernel, n_out, n_in),
+        out_shape=jax.ShapeDtypeStruct((n_in, frames, sub), BF16),
+        in_specs=whole_specs(2),
+        out_specs=pl.BlockSpec(memory_space=pltpu.VMEM),
+        scratch_shapes=[
+            blocks(2 * count), blocks(count), blocks(count), blocks(count - 1), blocks(count - 1),
+            dma(2 * count), dma(2 * count), dma(count), dma(count), dma(count - 1), dma(count - 1),
+            dma(n_in - 1), dma(n_in - 1),
+        ],
+        compiler_params=remote_params(3),
+    )(spread, hidden)
 
 
 def shards(
@@ -192,23 +499,14 @@
 
     gathered = lax.all_gather(slopes, "out", axis=0, tiled=True)
     partial_first = forward(gathered, None, first, live_first, weight_first, frames, n_in, sub)
-    summed_first = lax.psum_scatter(partial_first, "in", scatter_dimension=0, tiled=False)
-    hidden = jnp.tanh(summed_first + bias_first[None, :]).astype(BF16)
-
-    ordered = lax.all_gather(hidden, "out", axis=0, tiled=False)
+    hidden, ordered = hidden_layer(n_out, n_in, partial_first, bias_first)
+
     partial_second = forward(ordered, sub, second, live_second, weight_second, frames, n_in, sub)
-    summed_second = lax.psum_scatter(partial_second, "in", scatter_dimension=0, tiled=False)
-    estimate = jnp.tanh(summed_second + bias_second[None, :]).astype(BF16)
-    est32 = estimate.astype(F32)
-    delta_second = (cotangent.astype(F32) * (1.0 - est32 * est32)).astype(BF16)
-
-    rows_second = lax.all_gather(delta_second, "in", axis=0, tiled=False)
+    estimate, rows_second = estimate_layer(n_in, partial_second, bias_second, cotangent)
+
     spread = adjoint(rows_second, weight_second, second, live_second, n_out)
-    back = lax.psum_scatter(spread, "out", scatter_dimension=0, tiled=False).astype(F32)
+    rows_first = reduce_layer(n_out, n_in, spread, hidden)
     grad_second = weight_grad(ordered, sub, second, live_second, rows_second, KD2)
-    hid32 = hidden.astype(F32)
-    delta_first = (back * (1.0 - hid32 * hid32)).astype(BF16)
-    rows_first = lax.all_gather(delta_first, "in", axis=0, tiled=False)
     grad_first = weight_grad(gathered, None, first, live_first, rows_first, KD1)
     return (estimate, grad_first, grad_second)
 

time: 352 us -> 281 us (0.80)
  waiting for transfers between devices: 269 us -> 113 us
  Pallas kernels: 40.3 us -> 151 us
  blocking collectives: 15.8 us -> 0 us
  local copies, waits for them, and re-layouts: 7.46 us -> 2.45 us
  other arithmetic: 4.78 us -> 0 us
    pallas_call x0 -> x3, Pallas kernels: none -> 112 us  [the longest x1 50.8 us: reduce_layer(): pl.pallas_call(functools.partial(reduce_kernel, n_out, n_in), out_shape=j...]
    reduce_scatter x3 -> x0, waiting for transfers between devices: 104 us -> none  [the longest x1 64.5 us: shards(): lax.psum_scatter(spread, 'out', scatter_dimension=0, tiled=False)]
    all_gather x1 -> x0, waiting for transfers between devices: 51.5 us -> none  [shards(): ordered = lax.all_gather(hidden, 'out', axis=0, tiled=False)]
    all_gather x2 -> x0, blocking collectives: 15.8 us -> none  [the longest x1 8.71 us: shards(): rows_second = lax.all_gather(delta_second, 'in', axis=0, tiled=False)]
    unnamed x25 -> x14, local copies, waits for them, and re-layouts: 7.15 us -> 2.15 us
    convert_element_type x3 -> x0, other arithmetic: 4.78 us -> none  [the longest x1 1.88 us: shards(): delta_second = (cotangent.astype(F32) * (1.0 - est32 * est32)).astype(BF16)]
  transfers between devices with their start and end apart: 5 -> 1, of which waited for: 5 -> 1; matrix products, arithmetic and copies ran while one was open for 0% -> 0% of each run, Pallas kernels for 2% -> 0%
where the time goes in v2:
time: 281 us; the launch traced here: 280 us
  Pallas kernels  151 us (54%)
  waiting for transfers between devices  113 us (40%)
  between operations  14.1 us (5%)
    all_gather x1, waiting for transfers between devices, shards(): gathered = lax.all_gather(slopes, 'out', axis=0, tiled=True)  112 us
    pallas_call x1, Pallas kernels, reduce_layer(): pl.pallas_call(functools.partial(reduce_kernel, n_out, n_in), out_shape=j...  50.8 us
    pallas_call x1, Pallas kernels, hidden_layer(): pl.pallas_call(functools.partial(hidden_kernel, n_out, n_in), out_shape=(...  45.3 us
    pallas_call x2, Pallas kernels, forward(): pl.pallas_call(functools.partial(forward_kernel, slots), grid_spec=pltpu....  15.7 us
    pallas_call x2, Pallas kernels, weight_grad(): pl.pallas_call(functools.partial(grad_kernel, slots), grid_spec=pltpu.Pre...  15.6 us
    pallas_call x1, Pallas kernels, estimate_layer(): pl.pallas_call(functools.partial(estimate_kernel, n_in), out_shape=(jax.S...  15.6 us
    pallas_call x1, Pallas kernels, adjoint(): pl.pallas_call(functools.partial(adjoint_kernel, slots), grid_spec=pltpu....  7.72 us
  transfers between devices with their start and end apart: 1, of which 1 were waited for; matrix products, arithmetic and copies ran while one was open for 0% of the time, Pallas kernels for 0%

profile of v2, /device:TPU:0, one launch (start us, length us, event | category | flops | bytes accessed | tf_op | source)
XLA Modules:
  0.0 280.3 jit_solution(9194854540409082350)
XLA Ops:
  7.2 0.0 copy-start
  7.2 0.0 all-gather.2.cloned.1.call-start
  7.2 0.7 all-gather.2.cloned.1.call-update
  7.9 0.0 copy-done
  7.9 0.1 constant_dynamic-slice_fusion
  8.0 0.1 copy.16
  8.1 0.1 reshape.26.cols
  8.2 0.8 copy.15
  8.9 0.1 reshape.24.cols
  9.0 112.2 %all-gather.2.cloned.1.call-done.refs_0_.refs_1_.refs_2_.refs_3_.refs_4_.refs_5_.refs_6_.refs_7_ = bf16[128,81920]{1,0:T(8,128)(2,1)} async-done(((bf16[8,81920]{1,0:T(8,128)(2,1)}), bf16[128,81920]{1,0:T(8,128)(2,1)}) %all-gather.2.cloned.1.call-update) | async-done | bytes 20971536 | tf_op jit(solution)/shard_map/all_gather | solution.py:500
  121.2 0.7 copy-done.5
  121.8 8.7 %shard_map.121.partial = f32[2,128,1024]{2,1,0:T(8,128)S(1)} custom-call(s32[64]{0:T(128)S(1)} %reshape.26.cols, s32[8]{0:T(128)S(1)} %bitcast.9, bf16[128,81920]{1,0:T(8,128)(2,1)} %all-gather.2.cloned.1.call-done.refs_0_.refs_1_.refs_2_.refs_3_.refs_4_.refs_5_.refs_6_.refs_7_, ...), custom_call_target="tpu_custom_call" | custom-call | tf_op jit(solution)/shard_map/pallas_call | solution.py:121
  130.5 0.0 copy-done.3
  130.5 45.3 %shard_map.122 = (bf16[128,1024]{1,0:T(8,128)(2,1)S(1)}, bf16[16,128,1024]{2,1,0:T(8,128)(2,1)S(1)}) custom-call(f32[2,128,1024]{2,1,0:T(8,128)S(1)} %shard_map.121.partial, f32[1,1024]{1,0:T(1,128)S(1)} %bitcast.7), custom_call_target="tpu_custom_call" | custom-call | tf_op jit(solution)/shard_map/pallas_call | solution.py:418
  175.9 0.0 copy-done.2
  175.9 0.0 copy-start.1
  175.9 0.0 copy-start.4
  175.9 7.0 %shard_map.123.partial = f32[2,128,1024]{2,1,0:T(8,128)S(1)} custom-call(s32[32]{0:T(128)S(1)} %reshape.24.cols, s32[8]{0:T(128)S(1)} %bitcast.4, bf16[16,128,1024]{2,1,0:T(8,128)(2,1)S(1)} %get-tuple-element.7.refs_0_.refs_1_.refs_2_.refs_3_, bf16[16,128,1024]{2,1,0:T(8,128)(2,1)S(1)} %get-tuple-element.7.refs_0_.refs_1_.refs_2_.refs_3_, ...), custom_call_target="tpu_custom_call" | custom-call | tf_op jit(solution)/shard_map/pallas_call | solution.py:121
  183.0 15.6 %shard_map.124 = (bf16[128,1024]{1,0:T(8,128)(2,1)S(1)}, bf16[2,128,1024]{2,1,0:T(8,128)(2,1)S(1)}) custom-call(f32[2,128,1024]{2,1,0:T(8,128)S(1)} %shard_map.123.partial, f32[1,1024]{1,0:T(1,128)S(1)} %bitcast.8, bf16[128,1024]{1,0:T(8,128)(2,1)S(1)} %copy-done.1), custom_call_target="tpu_custom_call" | custom-call | tf_op jit(solution)/shard_map/pallas_call | solution.py:441
  198.6 6.1 %shard_map.128 = bf16[8,4,256,256]{3,2,1,0:T(8,128)(2,1)} custom-call(s32[32]{0:T(128)S(1)} %reshape.24.cols, s32[8]{0:T(128)S(1)} %bitcast.5, bf16[16,128,1024]{2,1,0:T(8,128)(2,1)S(1)} %get-tuple-element.7.refs_0_.refs_1_.refs_2_.refs_3_, bf16[16,128,1024]{2,1,0:T(8,128)(2,1)S(1)} %get-tuple-element.7.refs_0_.refs_1_.refs_2_.refs_3_, ...), custom_call_target="tpu_custom_call" | custom-call | flops 536870912 | bytes 6291456 | tf_op jit(solution)/shard_map/pallas_call | solution.py:137
  204.7 7.7 %shard_map.125.spread = bf16[16,128,1024]{2,1,0:T(8,128)(2,1)S(1)} custom-call(s32[32]{0:T(128)S(1)} %reshape.24.cols, s32[8]{0:T(128)S(1)} %bitcast.6, bf16[2,128,1024]{2,1,0:T(8,128)(2,1)S(1)} %get-tuple-element.9.delta.refs_4_, bf16[8,4,256,256]{3,2,1,0:T(8,128)(2,1)} %weight.1), custom_call_target="tpu_custom_call" | custom-call | tf_op jit(solution)/shard_map/pallas_call | solution.py:158
  212.4 50.8 %shard_map.126.refs_8_ = bf16[2,128,1024]{2,1,0:T(8,128)(2,1)S(1)} custom-call(bf16[16,128,1024]{2,1,0:T(8,128)(2,1)S(1)} %shard_map.125.spread, bf16[128,1024]{1,0:T(8,128)(2,1)S(1)} %get-tuple-element.10.hidden), custom_call_target="tpu_custom_call" | custom-call | tf_op jit(solution)/shard_map/pallas_call | solution.py:465
  263.3 9.5 %shard_map.127 = bf16[8,8,256,256]{3,2,1,0:T(8,128)(2,1)} custom-call(s32[64]{0:T(128)S(1)} %reshape.26.cols, s32[8]{0:T(128)S(1)} %bitcast.10, bf16[128,81920]{1,0:T(8,128)(2,1)} %all-gather.2.cloned.1.call-done.refs_0_.refs_1_.refs_2_.refs_3_.refs_4_.refs_5_.refs_6_.refs_7_, ...), custom_call_target="tpu_custom_call" | custom-call | flops 1073741824 | bytes 12582912 | tf_op jit(solution)/shard_map/pallas_call | solution.py:137
  272.7 0.7 copy.18
  (5 shorter events, 0.0 us)
Async XLA Ops:
  7.2 0.8 copy-start
  7.2 114.0 %all-gather.2.cloned.1.call-start = ((), (), s32[]{:S(2)}) async-start(), calls=%async_computation | async-start | bytes 22282240 | tf_op jit(solution)/shard_map/all_gather | solution.py:500
  121.2 0.7 copy-start.5
  121.8 8.7 %copy-start.3 = (f32[1024]{0:T(1024)S(1)}, f32[1024]{0:T(1024)}, u32[]{:S(2)}) copy-start(f32[1024]{0:T(1024)} %param.14) | copy-start | bytes 12292
  121.8 54.1 %copy-start.2 = (s32[8,1]{0,1:T(1,128)S(1)}, s32[8,1]{0,1:T(1,128)}, u32[]{:S(2)}) copy-start(s32[8,1]{0,1:T(1,128)} %param.16) | copy-start | bytes 100
  175.9 7.1 %copy-start.1 = (bf16[128,1024]{1,0:T(8,128)(2,1)S(1)}, bf16[128,1024]{1,0:T(8,128)(2,1)}, u32[]{:S(2)}) copy-start(bf16[128,1024]{1,0:T(8,128)(2,1)} %cotangent.1) | copy-start | bytes 786436
  175.9 7.1 %copy-start.4 = (f32[1024]{0:T(1024)S(1)}, f32[1024]{0:T(1024)}, u32[]{:S(2)}) copy-start(f32[1024]{0:T(1024)} %param.18) | copy-start | bytes 12292
Sparse Core Ops, SparseCore 0:
  9.6 111.5 all-gather.1

commit v3 on v2

--- a/solution.py
+++ b/solution.py
@@ -31,10 +31,15 @@
 
 
 def read_panel(ref):
-    if len(ref.shape) == 2:
-        return ref[...]
     parts = [ref[i] for i in range(ref.shape[0])]
     return parts[0] if len(parts) == 1 else jnp.concatenate(parts, axis=1)
+
+
+def slot_panel(panels, k):
+    if len(panels) > 1:
+        return read_panel(panels[k])
+    pieces, _, frames, width = panels[0].shape
+    return panels[0][:, k].astype(F32).reshape(pieces * frames, width).astype(BF16)
 
 
 def write_panel(ref, value):
@@ -44,23 +49,23 @@
 
 
 def forward_kernel(slots, cols, counts, *refs):
-    panels, weight, out = refs[:slots], refs[slots], refs[slots + 1]
+    panels, weight, out = refs[:-2], refs[-2], refs[-1]
     live = counts[pl.program_id(0)]
     total = None
     for k in range(slots):
-        term = jnp.dot(read_panel(panels[k]), weight[0, k], preferred_element_type=F32)
+        term = jnp.dot(slot_panel(panels, k), weight[0, k], preferred_element_type=F32)
         term = jnp.where(k < live, term, 0.0)
         total = term if total is None else total + term
     write_panel(out, total)
 
 
 def grad_kernel(slots, cols, counts, *refs):
-    panels, delta, out = refs[:slots], refs[slots], refs[slots + 1]
+    panels, delta, out = refs[:-2], refs[-2], refs[-1]
     live = counts[pl.program_id(0)]
     rows = read_panel(delta)
     for k in range(slots):
         term = lax.dot_general(
-            read_panel(panels[k]), rows, (((0,), (0,)), ((), ())), preferred_element_type=F32
+            slot_panel(panels, k), rows, (((0,), (0,)), ((), ())), preferred_element_type=F32
         )
         out[0, k] = jnp.where(k < live, term, 0.0).astype(out.dtype)
 
@@ -96,10 +101,12 @@
                 out[p] = total[p // per, :, at : at + sub].astype(out.dtype)
 
 
-def panel_specs(slots, frames, sub):
+def panel_specs(slots, frames, sub, inputs):
+    if sub is None:
+        pieces, _, own, _ = inputs.shape
+        return [pl.BlockSpec((pieces, slots, own, BLK), lambda r, cols, counts: (0, r, 0, 0))]
+
     def spec(k):
-        if sub is None:
-            return pl.BlockSpec((frames, BLK), lambda r, cols, counts: (0, cols[r * slots + k]))
         return pl.BlockSpec(
             panel_block(frames, sub),
             lambda r, cols, counts: panel_place(sub, cols[r * slots + k]),
@@ -123,12 +130,12 @@
         grid_spec=pltpu.PrefetchScalarGridSpec(
             num_scalar_prefetch=2,
             grid=(rows,),
-            in_specs=panel_specs(slots, frames, in_sub) + [weight_spec(slots)],
+            in_specs=panel_specs(slots, frames, in_sub, inputs) + [weight_spec(slots)],
             out_specs=row_spec(frames, sub),
         ),
         out_shape=jax.ShapeDtypeStruct((pieces, frames, sub), F32),
         compiler_params=params(),
-    )(cols, counts, *([inputs] * slots), weight)
+    )(cols, counts, *([inputs] * (1 if in_sub is None else slots)), weight)
 
 
 def weight_grad(inputs, in_sub, cols, counts, delta, slots):
@@ -139,7 +146,7 @@
         grid_spec=pltpu.PrefetchScalarGridSpec(
             num_scalar_prefetch=2,
             grid=(rows,),
-            in_specs=panel_specs(slots, frames, in_sub) + [row_spec(frames, sub)],
+            in_specs=panel_specs(slots, frames, in_sub, inputs) + [row_spec(frames, sub)],
             out_specs=weight_spec(slots),
         ),
         out_shape=jax.ShapeDtypeStruct((rows, slots, BLK, BLK), BF16),
@@ -149,7 +156,7 @@
             transcendentals=0,
         ),
         compiler_params=params(),
-    )(cols, counts, *([inputs] * slots), delta)
+    )(cols, counts, *([inputs] * (1 if in_sub is None else slots)), delta)
 
 
 def adjoint(delta, weight, cols, counts, out_pieces):
@@ -252,17 +259,7 @@
         copy.wait()
 
 
-def hidden_kernel(
-    n_out, n_in, partial, bias, hidden, ordered, leaving, arriving, in_send, in_recv, send, recv, own
-):
-    frames = hidden.shape[0]
-    greet(in_peers(n_in) + out_peers(n_out))
-    exchange_start(n_in, partial, leaving, arriving, in_send, in_recv)
-
-    def finish(at):
-        hidden[at, :] = jnp.tanh(exchanged(n_in, partial, arriving, bias, at)).astype(BF16)
-
-    by_rows(frames, finish)
+def gather_out(n_out, hidden, ordered, send, recv, own):
     me, outer, inner, core_peer, x_peer = out_place(n_out)
     count = n_out // SIDE
     copies = []
@@ -303,6 +300,20 @@
     keep.wait()
 
 
+def hidden_kernel(
+    n_out, n_in, partial, bias, hidden, ordered, leaving, arriving, in_send, in_recv, send, recv, own
+):
+    frames = hidden.shape[0]
+    greet(in_peers(n_in) + out_peers(n_out))
+    exchange_start(n_in, partial, leaving, arriving, in_send, in_recv)
+
+    def finish(at):
+        hidden[at, :] = jnp.tanh(exchanged(n_in, partial, arriving, bias, at)).astype(BF16)
+
+    by_rows(frames, finish)
+    gather_out(n_out, hidden, ordered, send, recv, own)
+
+
 def estimate_kernel(
     n_in, partial, bias, cotangent, estimate, rows, leaving, arriving, in_send, in_recv, send, recv
 ):
@@ -476,6 +487,187 @@
     )(spread, hidden)
 
 
+def slopes_kernel(n_out, cols, slopes, panels, packed, send, recv, own):
+    slots = packed.shape[1]
+    me, outer, inner, _, _ = out_place(n_out)
+    count = n_out // SIDE
+    greet([{"out": lax.rem(me + t, n_out)} for t in range(1, n_out)])
+
+    def pack(target):
+        def turn(i, carry):
+            for j in range(8):
+                at = i * 8 + j
+                packed[target, at] = slopes[cols[target * slots + at]]
+            return carry
+
+        lax.fori_loop(0, slots // 8, turn, 0)
+
+    copies = []
+    order = sorted(range(count), key=lambda t: -min(t, count - t))
+    for t in order:
+        for step in range(SIDE):
+            k = t * SIDE + step
+            if k == 0:
+                continue
+            target = lax.rem(outer + t, count) * SIDE + lax.rem(inner + step, SIDE)
+            pack(target)
+            copy = remote(
+                packed.at[target], panels.at[me], send.at[k], recv.at[k], {"out": target}
+            )
+            copy.start()
+            copies.append(copy)
+    pack(me)
+    keep = pltpu.make_async_copy(packed.at[me], panels.at[me], own)
+    keep.start()
+    for copy in copies:
+        copy.wait()
+    keep.wait()
+
+
+def slope_panels(n_out, slopes, cols):
+    frames = slopes.shape[0]
+    slots = cols.shape[0] // n_out
+    shape = (n_out, slots, frames, BLK)
+    return pl.pallas_call(
+        functools.partial(slopes_kernel, n_out),
+        out_shape=jax.ShapeDtypeStruct(shape, BF16),
+        in_specs=[pl.BlockSpec(memory_space=pltpu.SMEM), pl.BlockSpec(memory_space=pltpu.VMEM)],
+        out_specs=pl.BlockSpec(memory_space=pl.ANY),
+        scratch_shapes=[
+            pltpu.VMEM(shape, BF16), dma(n_out), dma(n_out), pltpu.SemaphoreType.DMA
+        ],
+        compiler_params=remote_params(4),
+    )(cols, slopes.reshape(frames, -1, BLK).transpose(1, 0, 2))
+
+
+def first_kernel(
+    n_out, n_in, cols, counts, slopes, weight_hbm, bias, hidden, ordered, kept,
+    packed, panels, weight, leaving, arriving, mine,
+    p_send, p_recv, w_sem, kept_sem, in_send, in_recv, send, recv, own,
+):
+    frames = hidden.shape[0]
+    rows, depth = weight.shape[:2]
+    chunk = panels.shape[2]
+    slots, per = chunk * n_in, chunk // depth
+    me, outer, inner, _, _ = out_place(n_out)
+    place = lax.axis_index("in")
+    count = n_out // SIDE
+    greet(in_peers(n_in) + [{"out": lax.rem(me + t, n_out)} for t in range(1, n_out)])
+    load = pltpu.make_async_copy(weight_hbm, weight, w_sem)
+    load.start()
+
+    def pack(into, h, target, at, piece):
+        def turn(i, carry):
+            for j in range(8):
+                k = i * 8 + j
+                into[h, at, k] = slopes[cols[target * slots + piece * chunk + k]]
+            return carry
+
+        lax.fori_loop(0, chunk // 8, turn, 0)
+
+    order = sorted(range(count), key=lambda t: -min(t, count - t))
+    copies = []
+    for h in range(n_in):
+        piece = lax.rem(place + 1 + h, n_in)
+        sent = []
+        for t in order:
+            for step in range(SIDE):
+                k = t * SIDE + step
+                if k == 0:
+                    continue
+                target = lax.rem(outer + t, count) * SIDE + lax.rem(inner + step, SIDE)
+                pack(packed, h, target, target, piece)
+                copy = remote(
+                    packed.at[h, target], panels.at[h, me], p_send.at[h, k], p_recv.at[h, k],
+                    {"out": target},
+                )
+                copy.start()
+                sent.append(copy)
+        pack(panels, h, me, me, piece)
+        copies.append(sent)
+
+    load.wait()
+    saves, exchanges = [], []
+    for h, peer in enumerate(in_peers(n_in) + [None]):
+        piece = lax.rem(place + 1 + h, n_in)
+        for copy in copies[h]:
+            copy.wait_recv()
+        save = pltpu.make_async_copy(
+            panels.at[h], kept.at[:, pl.ds(piece * chunk, chunk)], kept_sem.at[h]
+        )
+        save.start()
+        saves.append(save)
+        for j in range(per):
+            row = piece * per + j
+            live = counts[row]
+            total = None
+            for k in range(depth):
+                panel = panels[h, :, j * depth + k].astype(F32).reshape(frames, BLK).astype(BF16)
+                term = jnp.dot(panel, weight[row, k], preferred_element_type=F32)
+                term = jnp.where(k < live, term, 0.0)
+                total = term if total is None else total + term
+            if peer is None:
+                mine[:, j * BLK : (j + 1) * BLK] = total
+            else:
+                leaving[h, :, j * BLK : (j + 1) * BLK] = total.astype(BF16)
+        if peer is not None:
+            copy = remote(leaving.at[h], arriving.at[h], in_send.at[h], in_recv.at[h], peer)
+            copy.start()
+            exchanges.append(copy)
+    for copy in exchanges:
+        copy.wait_recv()
+
+    def finish(at):
+        total = mine[at, :]
+        for t in range(n_in - 1):
+            total = total + arriving[t, at, :].astype(F32)
+        hidden[at, :] = jnp.tanh(total + bias[...]).astype(BF16)
+
+    by_rows(frames, finish)
+    gather_out(n_out, hidden, ordered, send, recv, own)
+    for copy in sum(copies, []) + exchanges:
+        copy.wait_send()
+    for save in saves:
+        save.wait()
+
+
+def first_layer(n_out, n_in, slopes, cols, counts, weight, bias):
+    own_frames = slopes.shape[0]
+    frames, sub = own_frames * n_out, bias.shape[0]
+    slots = cols.shape[0] // n_out
+    split = (n_in, n_out, slots // n_in, own_frames, BLK)
+    smem = pl.BlockSpec(memory_space=pltpu.SMEM)
+    vmem = pl.BlockSpec(memory_space=pltpu.VMEM)
+    anywhere = pl.BlockSpec(memory_space=pl.ANY)
+    return pl.pallas_call(
+        functools.partial(first_kernel, n_out, n_in),
+        out_shape=(
+            jax.ShapeDtypeStruct((frames, sub), BF16),
+            jax.ShapeDtypeStruct((n_out, frames, sub), BF16),
+            jax.ShapeDtypeStruct((n_out, slots, own_frames, BLK), BF16),
+        ),
+        in_specs=[smem, smem, vmem, anywhere, vmem],
+        out_specs=(vmem, anywhere, anywhere),
+        scratch_shapes=[
+            pltpu.VMEM(split, BF16),
+            pltpu.VMEM(split, BF16),
+            pltpu.VMEM(weight.shape, BF16),
+            pltpu.VMEM((n_in - 1, frames, sub), BF16),
+            pltpu.VMEM((n_in - 1, frames, sub), BF16),
+            pltpu.VMEM((frames, sub), F32),
+            pltpu.SemaphoreType.DMA((n_in, n_out)),
+            pltpu.SemaphoreType.DMA((n_in, n_out)),
+            pltpu.SemaphoreType.DMA,
+            dma(n_in), dma(n_in - 1), dma(n_in - 1), dma(n_out), dma(n_out),
+            pltpu.SemaphoreType.DMA,
+        ],
+        compiler_params=remote_params(5),
+    )(
+        cols, counts, slopes.reshape(own_frames, -1, BLK).transpose(1, 0, 2), weight,
+        bias.reshape(1, -1),
+    )
+
+
 def shards(
     n_out,
     n_in,
@@ -493,13 +685,18 @@
     rows = weight_first.shape[0]
     frames = slopes.shape[0] * n_out
     sub = bias_first.shape[0]
-    first = lax.dynamic_slice_in_dim(cols_first, lax.axis_index("out") * rows, rows, 0).reshape(-1)
     second = cols_second.reshape(-1)
     live_first, live_second = count_first.reshape(-1), count_second.reshape(-1)
 
-    gathered = lax.all_gather(slopes, "out", axis=0, tiled=True)
-    partial_first = forward(gathered, None, first, live_first, weight_first, frames, n_in, sub)
-    hidden, ordered = hidden_layer(n_out, n_in, partial_first, bias_first)
+    all_cols = cols_first.reshape(-1)
+    if sub >= BLK:
+        hidden, ordered, panels = first_layer(
+            n_out, n_in, slopes, all_cols, live_first, weight_first, bias_first
+        )
+    else:
+        panels = slope_panels(n_out, slopes, all_cols)
+        partial_first = forward(panels, None, second, live_first, weight_first, frames, n_in, sub)
+        hidden, ordered = hidden_layer(n_out, n_in, partial_first, bias_first)
 
     partial_second = forward(ordered, sub, second, live_second, weight_second, frames, n_in, sub)
     estimate, rows_second = estimate_layer(n_in, partial_second, bias_second, cotangent)
@@ -507,7 +704,7 @@
     spread = adjoint(rows_second, weight_second, second, live_second, n_out)
     rows_first = reduce_layer(n_out, n_in, spread, hidden)
     grad_second = weight_grad(ordered, sub, second, live_second, rows_second, KD2)
-    grad_first = weight_grad(gathered, None, first, live_first, rows_first, KD1)
+    grad_first = weight_grad(panels, None, second, live_first, rows_first, KD1)
     return (estimate, grad_first, grad_second)
 
 

time: 281 us -> 236 us (0.84)
  waiting for transfers between devices: 113 us -> 0 us
  Pallas kernels: 151 us -> 230 us
  between operations: 14.1 us -> 0.75 us
    all_gather x1 -> x0, waiting for transfers between devices: 112 us -> none  [shards(): gathered = lax.all_gather(slopes, 'out', axis=0, tiled=True)]
    pallas_call x1, Pallas kernels: 45.3 us -> 144 us  [first_layer(): pl.pallas_call(functools.partial(first_kernel, n_out, n_in), out_shape=(j...]
    pallas_call x1, Pallas kernels: 50.8 us -> 41.4 us  [reduce_layer(): pl.pallas_call(functools.partial(reduce_kernel, n_out, n_in), out_shape=j...]
    pallas_call x2 -> x1, Pallas kernels: 15.7 us -> 7.05 us  [forward(): pl.pallas_call(functools.partial(forward_kernel, slots), grid_spec=pltpu....]
  transfers between devices with their start and end apart: 1 -> 0, of which waited for: 1 -> 0; matrix products, arithmetic and copies ran while one was open for 0% -> 0% of each run, Pallas kernels for 0% -> 0%
where the time goes in v3:
time: 236 us
  Pallas kernels  230 us (97%)
  local copies, waits for them, and re-layouts  5.1 us (2%)
    pallas_call x1, Pallas kernels, first_layer(): pl.pallas_call(functools.partial(first_kernel, n_out, n_in), out_shape=(j...  144 us
    pallas_call x1, Pallas kernels, reduce_layer(): pl.pallas_call(functools.partial(reduce_kernel, n_out, n_in), out_shape=j...  41.4 us
    pallas_call x1, Pallas kernels, estimate_layer(): pl.pallas_call(functools.partial(estimate_kernel, n_in), out_shape=(jax.S...  16.9 us
    pallas_call x2, Pallas kernels, weight_grad(): pl.pallas_call(functools.partial(grad_kernel, slots), grid_spec=pltpu.Pre...  13.1 us
    pallas_call x1, Pallas kernels, adjoint(): pl.pallas_call(functools.partial(adjoint_kernel, slots), grid_spec=pltpu....  7.73 us
    pallas_call x1, Pallas kernels, forward(): pl.pallas_call(functools.partial(forward_kernel, slots), grid_spec=pltpu....  7.05 us
    unnamed x19, local copies, waits for them, and re-layouts  4.93 us

profile of v3, /device:TPU:0, one launch (start us, length us, event | category | flops | bytes accessed | tf_op | source)
XLA Modules:
  0.0 235.8 jit_solution(12220707916094886936)
XLA Ops:
  0.6 0.8 copy.14
  1.4 0.1 reshape.27.cols
  1.5 0.8 copy.15
  2.3 0.1 reshape.29.cols
  2.4 0.0 copy-start.1
  2.4 1.3 copy-done.1
  3.7 0.7 copy-done.4
  4.4 0.7 copy-done.6
  5.0 143.7 %shard_map.121 = (bf16[128,1024]{1,0:T(8,128)(2,1)S(1)}, bf16[16,128,1024]{2,1,0:T(8,128)(2,1)S(1)}, bf16[16,64,8,256]{3,2,1,0:T(8,128)(2,1)}) custom-call(s32[1024]{0:T(1024)S(1)} %reshape.29.cols, s32[8]{0:T(128)S(1)} %bitcast.13, bf16[320,8,256]{2,1,0:T(8,128)(2,1)S(1)} %bitcast.7, bf16[8,8,256,256]{3,2,1,0:T(8,128)(2,1)} %weight_hbm.1, ...), custom_call_target="tpu_custom_call" | custom-call | tf_op jit(solution)/shard_map/pallas_call | solution.py:642
  148.7 0.0 copy-done.3
  148.7 0.0 copy-start.2
  148.7 0.0 copy-start.5
  148.7 7.0 %shard_map.122.partial = f32[2,128,1024]{2,1,0:T(8,128)S(1)} custom-call(s32[32]{0:T(128)S(1)} %reshape.27.cols, s32[8]{0:T(128)S(1)} %bitcast.8, bf16[16,128,1024]{2,1,0:T(8,128)(2,1)S(1)} %get-tuple-element.8.refs_0_.refs_1_.refs_2_.refs_3_, bf16[16,128,1024]{2,1,0:T(8,128)(2,1)S(1)} %get-tuple-element.8.refs_0_.refs_1_.refs_2_.refs_3_, ...), custom_call_target="tpu_custom_call" | custom-call | tf_op jit(solution)/shard_map/pallas_call | solution.py:128
  155.8 0.0 copy-done.2
  155.8 0.0 copy-done.5
  155.8 16.9 %shard_map.123 = (bf16[128,1024]{1,0:T(8,128)(2,1)S(1)}, bf16[2,128,1024]{2,1,0:T(8,128)(2,1)S(1)}) custom-call(f32[2,128,1024]{2,1,0:T(8,128)S(1)} %shard_map.122.partial, f32[1,1024]{1,0:T(1,128)S(1)} %bitcast.12, bf16[128,1024]{1,0:T(8,128)(2,1)S(1)} %copy-done.2), custom_call_target="tpu_custom_call" | custom-call | tf_op jit(solution)/shard_map/pallas_call | solution.py:452
  172.7 6.1 %shard_map.127 = bf16[8,4,256,256]{3,2,1,0:T(8,128)(2,1)} custom-call(s32[32]{0:T(128)S(1)} %reshape.27.cols, s32[8]{0:T(128)S(1)} %bitcast.9, bf16[16,128,1024]{2,1,0:T(8,128)(2,1)S(1)} %get-tuple-element.8.refs_0_.refs_1_.refs_2_.refs_3_, bf16[16,128,1024]{2,1,0:T(8,128)(2,1)S(1)} %get-tuple-element.8.refs_0_.refs_1_.refs_2_.refs_3_, ...), custom_call_target="tpu_custom_call" | custom-call | flops 536870912 | bytes 6291456 | tf_op jit(solution)/shard_map/pallas_call | solution.py:144
  178.8 7.7 %shard_map.124.spread = bf16[16,128,1024]{2,1,0:T(8,128)(2,1)S(1)} custom-call(s32[32]{0:T(128)S(1)} %reshape.27.cols, s32[8]{0:T(128)S(1)} %bitcast.10, bf16[2,128,1024]{2,1,0:T(8,128)(2,1)S(1)} %get-tuple-element.11.delta.refs_4_, bf16[8,4,256,256]{3,2,1,0:T(8,128)(2,1)} %weight.1), custom_call_target="tpu_custom_call" | custom-call | tf_op jit(solution)/shard_map/pallas_call | solution.py:165
  186.6 0.0 copy-start.7
  186.6 41.4 %shard_map.125.refs_1_ = bf16[2,128,1024]{2,1,0:T(8,128)(2,1)S(1)} custom-call(bf16[16,128,1024]{2,1,0:T(8,128)(2,1)S(1)} %shard_map.124.spread, bf16[128,1024]{1,0:T(8,128)(2,1)S(1)} %get-tuple-element.12.hidden), custom_call_target="tpu_custom_call" | custom-call | tf_op jit(solution)/shard_map/pallas_call | solution.py:476
  228.0 0.0 copy-done
  228.0 0.0 copy-done.7
  228.0 7.0 %shard_map.126 = bf16[8,8,256,256]{3,2,1,0:T(8,128)(2,1)} custom-call(s32[32]{0:T(128)S(1)} %reshape.27.cols, s32[8]{0:T(128)S(1)} %bitcast.14, bf16[16,64,8,256]{3,2,1,0:T(8,128)(2,1)S(1)} %copy-done, bf16[2,128,1024]{2,1,0:T(8,128)(2,1)S(1)} %shard_map.125.refs_1_), custom_call_target="tpu_custom_call" | custom-call | flops 1073741824 | bytes 12582912 | tf_op jit(solution)/shard_map/pallas_call | solution.py:144
  235.1 0.7 copy.17
  (4 shorter events, 0.0 us)
Async XLA Ops:
  2.4 1.3 copy-start.1
  3.7 0.7 copy-start.4
  4.4 0.7 copy-start.6
  5.0 143.7 %copy-start.3 = (s32[8,1]{0,1:T(1,128)S(1)}, s32[8,1]{0,1:T(1,128)}, u32[]{:S(2)}) copy-start(s32[8,1]{0,1:T(1,128)} %param.16) | copy-start | bytes 100
  148.7 7.1 %copy-start.2 = (bf16[128,1024]{1,0:T(8,128)(2,1)S(1)}, bf16[128,1024]{1,0:T(8,128)(2,1)}, u32[]{:S(2)}) copy-start(bf16[128,1024]{1,0:T(8,128)(2,1)} %cotangent.1) | copy-start | bytes 786436
  148.7 7.1 %copy-start.5 = (f32[1024]{0:T(1024)S(1)}, f32[1024]{0:T(1024)}, u32[]{:S(2)}) copy-start(f32[1024]{0:T(1024)} %param.18) | copy-start | bytes 12292
  186.6 41.5 %copy-start = (bf16[16,64,8,256]{3,2,1,0:T(8,128)(2,1)S(1)}, bf16[16,64,8,256]{3,2,1,0:T(8,128)(2,1)}, u32[]{:S(2)}) copy-start(bf16[16,64,8,256]{3,2,1,0:T(8,128)(2,1)} %get-tuple-element.10.refs_0_) | copy-start | bytes 12582916
  186.6 41.5 %copy-start.7 = (s32[8,1]{0,1:T(1,128)S(1)}, s32[8,1]{0,1:T(1,128)}, u32[]{:S(2)}) copy-start(s32[8,1]{0,1:T(1,128)} %param.12) | copy-start | bytes 100
